TPU v7x, 256 devices: a whole 4x4x8 slice. The times are simulated.
256 devices in a mesh: leaf: 64 (over y, z, core), rhs: 4 (over x).
Axes of the slice: x: 4, y: 4, z: 8, core: 2. Of those that a mesh axis runs over, the one named last changes fastest.
Arguments:
- leaf_right: float32 [2048, 256, 128], P('leaf', 'rhs'), may hold values from -6 to 6
- upper_right: float32 [128, 256, 128], P('leaf', 'rhs'), may hold values from -6 to 6
- leaf_inverse: bfloat16 [2048, 128, 128], P(('leaf', 'rhs')), as said below
- upper_inverse: bfloat16 [128, 128, 128], P('leaf'), as said below
- update_blocks: bfloat16 [16384, 128, 128], P('leaf'), may hold values from -0.046875 to 0.046875
- block_target: int32 [16384, 1], P('leaf'), may hold values from 0 to 127; in each aligned block of 256 rows (0 to 255, 256 to 511, ...) at most 4 rows name the same one
- upper_place: int32 [128], replicated, may hold values from 0 to 127, each once
Outputs:
- leaf_solution: float32 [2048, 256, 128], P('leaf', 'rhs')
- upper_solution: float32 [128, 256, 128], P('leaf', 'rhs')
Inputs may be any that keep to these rules, and one draw needn't show every extreme that they name: `leaf_inverse`: lower triangular blocks, diagonal entries between 0.6 and 1.4. `upper_inverse`: lower triangular blocks, diagonal entries between 0.6 and 1.4. `block_target`: among the 256 blocks of one device no upper supernode is named more than 4 times, a bound that some block reaches. `upper_place`: each row of the upper arrays holds exactly one upper supernode.
All inputs are finite; a program needn't handle non-finite values.
Results may differ from a plain program's by a relative error of at most 0.0049.
Values may be sent and summed in bfloat16 or wider, within the bound.
A program may use at most 64 MiB of HBM per device.

v0:
```python
import jax
import jax.numpy as jnp
from jax import lax
from jax.sharding import PartitionSpec as P


def on_device(
    leaf_right, upper_right, leaf_inverse, upper_inverse, update_blocks, block_target, upper_place
):
    inverse_mine = lax.all_gather(leaf_inverse, "rhs", axis=0, tiled=True)
    leaf_rounded = leaf_right.astype(jnp.bfloat16)
    leaf_forward = jnp.einsum(
        "ncw,nvw->ncv", leaf_rounded, inverse_mine, preferred_element_type=jnp.float32
    )
    leaf_half = leaf_forward.astype(jnp.bfloat16)
    leaf_count, columns, width = leaf_forward.shape
    block_count = update_blocks.shape[0]
    per_leaf = block_count // leaf_count
    grouped = update_blocks.reshape(leaf_count, per_leaf, width, width)
    updates = jnp.einsum("ncw,nbvw->nbcv", leaf_half, grouped, preferred_element_type=jnp.float32)
    updates = updates.reshape(block_count, columns, width)
    upper_total = upper_place.shape[0]
    table = jnp.arange(upper_total, dtype=jnp.int32)
    position = jnp.sum(jnp.where(block_target == table[None, :], upper_place[None, :], 0), axis=1)
    upper_rows = upper_right.shape[0]
    local_index = position
    inside = (local_index >= 0) & (local_index < upper_rows * lax.axis_size("leaf"))
    local_index = jnp.where(inside, local_index, upper_rows * lax.axis_size("leaf"))
    upper_sums = lax.psum_scatter(
        jax.ops.segment_sum(updates, local_index, num_segments=upper_rows * lax.axis_size("leaf")),
        "leaf",
        scatter_dimension=0,
        tiled=True,
    )
    upper_rounded = (upper_right - upper_sums).astype(jnp.bfloat16)
    upper_half = jnp.einsum(
        "pcw,pvw->pcv", upper_rounded, upper_inverse, preferred_element_type=jnp.float32
    ).astype(jnp.bfloat16)
    upper_solution = jnp.einsum(
        "pcw,pwv->pcv", upper_half, upper_inverse, preferred_element_type=jnp.float32
    )
    upper_sent = upper_solution.astype(jnp.bfloat16)
    solved_table = lax.all_gather(upper_sent, "leaf", axis=0, tiled=True)
    chosen = jnp.take(solved_table, position, axis=0)
    corrections = jnp.einsum(
        "kcv,kvw->kcw", chosen, update_blocks, preferred_element_type=jnp.float32
    )
    corrections = corrections.reshape(leaf_count, per_leaf, columns, width).sum(axis=1)
    leaf_back = (leaf_forward - corrections).astype(jnp.bfloat16)
    leaf_solution = jnp.einsum(
        "ncw,nwv->ncv", leaf_back, inverse_mine, preferred_element_type=jnp.float32
    )
    return (leaf_solution, upper_solution)


def solution(mesh):
    return jax.shard_map(
        on_device,
        mesh=mesh,
        in_specs=(
            P("leaf", "rhs", None),
            P("leaf", "rhs", None),
            P(("leaf", "rhs"), None, None),
            P("leaf", None, None),
            P("leaf", None, None),
            P("leaf", None),
            P(),
        ),
        out_specs=(P("leaf", "rhs", None), P("leaf", "rhs", None)),
        check_vma=False,
    )
```

profile of v0, /device:TPU:1, one launch (start us, length us, event | category | flops | bytes accessed | tf_op | source)
XLA Modules:
  0.0 338.4 jit_solution(17346281940933567968)
XLA Ops:
  7.2 0.0 copy-start
  7.2 0.0 all-gather.3.cloned.1.call-start
  7.2 0.7 all-gather.3.cloned.1.call-update
  7.9 0.0 reduce-scatter.2.cloned.1.call-start
  8.0 0.9 select_reduce_fusion
  8.8 30.4 %all-gather.3.cloned.1.call-done = bf16[32,128,128]{2,1,0:T(8,128)(2,1)} async-done(((bf16[8,128,128]{2,1,0:T(8,128)(2,1)}), bf16[32,128,128]{2,1,0:T(8,128)(2,1)}) %all-gather.3.cloned.1.call-update) | async-done | bytes 1048592 | tf_op jit(solution)/shard_map/all_gather | solution.py:10
  39.2 2.3 fusion.11
  41.6 9.6 %fusion.8 = f32[32,64,8,128]{3,1,2,0:T(8,128)} fusion(bf16[32,8,128,128]{3,2,1,0:T(8,128)(2,1)} %bitcast.22, f32[32,64,128]{2,1,0:T(8,128)S(1)} %fusion.11), kind=kOutput, calls=%fused_computation.11 | convolution fusion | flops 537133056 | bytes 17825792 | tf_op jit(solution)/shard_map/ncw,nbvw->nbcv/dot_general | solution.py:20
  51.2 2.5 broadcast_in_dim.33
  53.7 39.9 %scatter_fusion = f32[128,64,128]{2,1,0:T(8,128)} fusion(f32[128,64,128]{2,1,0:T(8,128)} %broadcast_in_dim.33, s32[256]{0:T(256)S(1)} %bitcast.23, f32[256,64,128]{2,1,0:T(8,128)} %bitcast.21), kind=kCustom, calls=%fused_computation.1 | custom fusion | flops 2097152 | bytes 25166848 | tf_op jit(solution)/shard_map/scatter-add | solution.py:30
  93.6 0.0 copy-start.2
  93.6 0.0 reduce-scatter.2.cloned.1.call-update
  93.6 0.0 all-gather.5.cloned.1.call-start
  93.7 140.1 %reduce-scatter.2.cloned.1.call-done = f32[2,64,128]{2,1,0:T(8,128)} async-done(((f32[128,64,128]{2,1,0:T(8,128)}), f32[2,64,128]{2,1,0:T(8,128)}) %reduce-scatter.2.cloned.1.call-update) | async-done | bytes 65552 | tf_op jit(solution)/shard_map/reduce_scatter | solution.py:29
  233.8 0.0 copy-done
  233.8 0.0 copy-done.2
  233.8 1.7 fusion.14
  235.5 0.0 all-gather.5.cloned.1.call-update
  235.6 83.0 %all-gather.5.cloned.1.call-done = bf16[128,64,128]{2,1,0:T(8,128)(2,1)} async-done(((bf16[2,64,128]{2,1,0:T(8,128)(2,1)}), bf16[128,64,128]{2,1,0:T(8,128)(2,1)}) %all-gather.5.cloned.1.call-update) | async-done | bytes 2097168 | tf_op jit(solution)/shard_map/all_gather | solution.py:43
  318.6 4.6 %gather_fusion = bf16[256,64,128]{2,1,0:T(8,128)(2,1)} fusion(bf16[128,64,128]{2,1,0:T(8,128)(2,1)} %all-gather.5.cloned.1.call-done, s32[1024]{0:T(1024)S(1)} %pad_clamp_fusion), kind=kCustom, calls=%fused_computation | custom fusion | bytes 8389632 | tf_op jit(solution)/shard_map/jit(_take)/gather | solution.py:44
  323.3 0.0 copy-start.1
  323.3 7.2 %bitcast_reduce_fusion = f32[32,64,128]{2,1,0:T(8,128)S(1)} fusion(bf16[256,128,128]{2,1,0:T(8,128)(2,1)} %param.11, bf16[256,64,128]{2,1,0:T(8,128)(2,1)} %gather_fusion, pred[256]{0:T(512)(128)(4,1)S(1)} %compare_and_fusion), kind=kOutput, calls=%fused_computation.2 | convolution fusion | flops 540803072 | bytes 13631744 | tf_op jit(solution)/shard_map/kcv,kvw->kcw/dot_general | solution.py:45
  330.4 0.0 copy-done.1
  330.4 1.4 fusion.7
  (3 shorter events, 0.0 us)
Async XLA Ops:
  7.2 226.6 %copy-start = (bf16[2,128,128]{2,1,0:T(8,128)(2,1)S(1)}, bf16[2,128,128]{2,1,0:T(8,128)(2,1)}, u32[]{:S(2)}) copy-start(bf16[2,128,128]{2,1,0:T(8,128)(2,1)} %param.10) | copy-start | bytes 196612
  7.2 32.1 %all-gather.3.cloned.1.call-start = ((), (), s32[]{:S(2)}) async-start(), calls=%async_computation.1 | async-start | bytes 1310720 | tf_op jit(solution)/shard_map/all_gather | solution.py:10
  7.9 225.9 %reduce-scatter.2.cloned.1.call-start = ((), (), s32[]{:S(2)}) async-start(), calls=%async_computation.2 | async-start | bytes 4259840 | tf_op jit(solution)/shard_map/reduce_scatter | solution.py:29
  93.6 140.2 %copy-start.2 = (f32[2,64,128]{2,1,0:T(8,128)S(1)}, f32[2,64,128]{2,1,0:T(8,128)}, u32[]{:S(2)}) copy-start(f32[2,64,128]{2,1,0:T(8,128)} %param.8) | copy-start | bytes 196612
  93.6 225.0 %all-gather.5.cloned.1.call-start = ((), (), s32[]{:S(2)}) async-start(), calls=%async_computation.3 | async-start | bytes 2129920 | tf_op jit(solution)/shard_map/all_gather | solution.py:43
  323.3 7.2 %copy-start.1 = (bf16[32,128,128]{2,1,0:T(8,128)(2,1)S(1)}, bf16[32,128,128]{2,1,0:T(8,128)(2,1)}, u32[]{:S(2)}) copy-start(bf16[32,128,128]{2,1,0:T(8,128)(2,1)} %all-gather.3.cloned.1.call-done) | copy-start | bytes 3145732
Sparse Core Ops, SparseCore 0:
  9.8 29.3 all-gather.2
  93.8 139.9 reduce-scatter.1
  237.5 81.0 all-gather.4
where the time goes:
time: 339 us; the launch traced here: 338 us
  waiting for transfers between devices  254 us (75%)
  other arithmetic  40.8 us (12%)
  matrix products  22.3 us (7%)
  between operations  13.8 us (4%)
  local copies, waits for them, and re-layouts  7.11 us (2%)
    reduce_scatter x1, waiting for transfers between devices, on_device(): lax.psum_scatter(jax.ops.segment_sum(updates, local_index, num_segments=u...  140 us
    all_gather x1, waiting for transfers between devices, on_device(): solved_table = lax.all_gather(upper_sent, 'leaf', axis=0, tiled=True)  83 us
    scatter-add x1, other arithmetic, on_device(): jax.ops.segment_sum(updates, local_index, num_segments=upper_rows * lax.a...  39.9 us
    all_gather x1, waiting for transfers between devices, on_device(): inverse_mine = lax.all_gather(leaf_inverse, 'rhs', axis=0, tiled=True)  30.4 us
    dot_general x1, matrix products, on_device(): jnp.einsum('ncw,nbvw->nbcv', leaf_half, grouped, preferred_element_type=j...  9.63 us
    dot_general x1, matrix products, on_device(): jnp.einsum('kcv,kvw->kcw', chosen, update_blocks, preferred_element_type=...  7.16 us
  transfers between devices with their start and end apart: 3, of which 3 were waited for; matrix products, arithmetic and copies ran while one was open for 0% of the time, Pallas kernels for 0%

commit v1 on v0

--- a/solution.py
+++ b/solution.py
@@ -7,7 +7,12 @@
 def on_device(
     leaf_right, upper_right, leaf_inverse, upper_inverse, update_blocks, block_target, upper_place
 ):
-    inverse_mine = lax.all_gather(leaf_inverse, "rhs", axis=0, tiled=True)
+    ring = [leaf_inverse]
+    for hop in range(3):
+        ring.append(lax.ppermute(ring[-1], "rhs", [(dev, (dev + 1) % 4) for dev in range(4)]))
+    inverse_mine = jnp.roll(
+        jnp.concatenate(ring[::-1], axis=0), (lax.axis_index("rhs") + 1) * ring[0].shape[0], axis=0
+    )
     leaf_rounded = leaf_right.astype(jnp.bfloat16)
     leaf_forward = jnp.einsum(
         "ncw,nvw->ncv", leaf_rounded, inverse_mine, preferred_element_type=jnp.float32

time: 339 us -> 332 us (0.979)
  waiting for transfers between devices: 254 us -> 243 us
  starting transfers between devices: 0.12 us -> 4.71 us
    all_gather x1 -> x0, waiting for transfers between devices: 30.4 us -> none  [on_device(): inverse_mine = lax.all_gather(leaf_inverse, 'rhs', axis=0, tiled=True)]
    ppermute x0 -> x3, waiting for transfers between devices: none -> 15.4 us  [on_device(): lax.ppermute(ring[-1], 'rhs', [(dev, (dev + 1) % 4) for dev in range(4)])]
    reduce_scatter x1, waiting for transfers between devices: 140 us -> 145 us  [on_device(): lax.psum_scatter(jax.ops.segment_sum(updates, local_index, num_segments=u...]
    ppermute x0 -> x3, starting transfers between devices: none -> 4.63 us  [on_device(): lax.ppermute(ring[-1], 'rhs', [(dev, (dev + 1) % 4) for dev in range(4)])]
  transfers between devices with their start and end apart: 3 -> 5, of which waited for: 3 -> 5; matrix products, arithmetic and copies ran while one was open for 0% -> 0% of each run, Pallas kernels for 0% -> 0%
where the time goes in v1:
time: 332 us
  waiting for transfers between devices  243 us (73%)
  other arithmetic  40.3 us (12%)
  matrix products  20.7 us (6%)
  between operations  14.2 us (4%)
  local copies, waits for them, and re-layouts  8.35 us (3%)
  starting transfers between devices  4.71 us (1%)
    reduce_scatter x1, waiting for transfers between devices, on_device(): lax.psum_scatter(jax.ops.segment_sum(updates, local_index, num_segments=u...  145 us
    all_gather x1, waiting for transfers between devices, on_device(): solved_table = lax.all_gather(upper_sent, 'leaf', axis=0, tiled=True)  83.1 us
    scatter-add x1, other arithmetic, on_device(): jax.ops.segment_sum(updates, local_index, num_segments=upper_rows * lax.a...  39.4 us
    ppermute x3, waiting for transfers between devices, on_device(): lax.ppermute(ring[-1], 'rhs', [(dev, (dev + 1) % 4) for dev in range(4)])  15.4 us
    dot_general x1, matrix products, on_device(): jnp.einsum('ncw,nbvw->nbcv', leaf_half, grouped, preferred_element_type=j...  9.63 us
    dot_general x1, matrix products, on_device(): jnp.einsum('kcv,kvw->kcw', chosen, update_blocks, preferred_element_type=...  7.1 us
  transfers between devices with their start and end apart: 5, of which 5 were waited for; matrix products, arithmetic and copies ran while one was open for 0% of the time, Pallas kernels for 0%

profile of v1, /device:TPU:1, one launch (start us, length us, event | category | flops | bytes accessed | tf_op | source)
XLA Modules:
  0.0 331.6 jit_solution(13001336889936337749)
XLA Ops:
  7.2 0.0 copy-start
  7.2 0.0 copy-start.2
  7.2 0.0 reduce-scatter.2.cloned.1.call-start
  7.2 2.1 collective-permute-start
  9.4 5.2 %collective-permute-done = bf16[8,128,128]{2,1,0:T(8,128)(2,1)S(1)} collective-permute-done((bf16[8,128,128]{2,1,0:T(8,128)(2,1)}, bf16[8,128,128]{2,1,0:T(8,128)(2,1)S(1)}, u32[]{:S(2)}, u32[]{:S(2)}) %collective-permute-start) | collective-permute-done | bytes 262176 | tf_op jit(solution)/shard_map/ppermute | solution.py:12
  14.6 1.9 collective-permute-start.1
  16.5 5.3 %collective-permute-done.1 = bf16[8,128,128]{2,1,0:T(8,128)(2,1)S(1)} collective-permute-done((bf16[8,128,128]{2,1,0:T(8,128)(2,1)S(1)}, bf16[8,128,128]{2,1,0:T(8,128)(2,1)S(1)}, u32[]{:S(2)}, u32[]{:S(2)}) %collective-permute-start.1) | collective-permute-done | bytes 262176 | tf_op jit(solution)/shard_map/ppermute | solution.py:12
  21.8 0.7 collective-permute-start.2
  22.4 0.9 select_reduce_fusion
  23.3 0.0 copy-start.1
  23.3 4.9 %collective-permute-done.2 = bf16[8,128,128]{2,1,0:T(8,128)(2,1)S(1)} collective-permute-done((bf16[8,128,128]{2,1,0:T(8,128)(2,1)S(1)}, bf16[8,128,128]{2,1,0:T(8,128)(2,1)S(1)}, u32[]{:S(2)}, u32[]{:S(2)}) %collective-permute-start.2) | collective-permute-done | bytes 262176 | tf_op jit(solution)/shard_map/ppermute | solution.py:12
  28.3 1.0 constant_dynamic-update-slice_fusion.4
  29.4 0.0 copy-done.2
  29.5 0.0 copy-done.1
  29.5 0.8 convolution_bitcast_fusion
  30.3 9.6 %fusion.10 = f32[32,64,8,128]{3,1,2,0:T(8,128)} fusion(bf16[32,8,128,128]{3,2,1,0:T(8,128)(2,1)} %bitcast.22, f32[32,64,128]{2,1,0:T(8,128)S(1)} %convolution_bitcast_fusion), kind=kOutput, calls=%fused_computation.14 | convolution fusion | flops 537133056 | bytes 17825792 | tf_op jit(solution)/shard_map/ncw,nbvw->nbcv/dot_general | solution.py:25
  40.0 2.5 broadcast_in_dim.33
  42.4 39.4 %scatter_fusion = f32[128,64,128]{2,1,0:T(8,128)} fusion(f32[128,64,128]{2,1,0:T(8,128)} %broadcast_in_dim.33, s32[256]{0:T(256)S(1)} %bitcast.23, f32[256,64,128]{2,1,0:T(8,128)} %bitcast.21), kind=kCustom, calls=%fused_computation.1 | custom fusion | flops 2097152 | bytes 25166848 | tf_op jit(solution)/shard_map/scatter-add | solution.py:35
  81.8 0.0 copy-start.3
  81.8 0.0 reduce-scatter.2.cloned.1.call-update
  81.8 0.0 all-gather.2.cloned.1.call-start
  81.9 144.8 %reduce-scatter.2.cloned.1.call-done = f32[2,64,128]{2,1,0:T(8,128)} async-done(((f32[128,64,128]{2,1,0:T(8,128)}), f32[2,64,128]{2,1,0:T(8,128)}) %reduce-scatter.2.cloned.1.call-update) | async-done | bytes 65552 | tf_op jit(solution)/shard_map/reduce_scatter | solution.py:34
  226.7 0.0 copy-done
  226.7 0.0 copy-done.3
  226.7 1.7 fusion.17
  228.5 0.0 all-gather.2.cloned.1.call-update
  228.5 83.1 %all-gather.2.cloned.1.call-done = bf16[128,64,128]{2,1,0:T(8,128)(2,1)} async-done(((bf16[2,64,128]{2,1,0:T(8,128)(2,1)}), bf16[128,64,128]{2,1,0:T(8,128)(2,1)}) %all-gather.2.cloned.1.call-update) | async-done | bytes 2097168 | tf_op jit(solution)/shard_map/all_gather | solution.py:48
  311.6 4.6 %gather_fusion = bf16[256,64,128]{2,1,0:T(8,128)(2,1)} fusion(bf16[128,64,128]{2,1,0:T(8,128)(2,1)} %all-gather.2.cloned.1.call-done, s32[1024]{0:T(1024)S(1)} %pad_clamp_fusion), kind=kCustom, calls=%fused_computation | custom fusion | bytes 8389632 | tf_op jit(solution)/shard_map/jit(_take)/gather | solution.py:49
  316.2 7.1 %bitcast_reduce_fusion = f32[32,64,128]{2,1,0:T(8,128)S(1)} fusion(bf16[256,128,128]{2,1,0:T(8,128)(2,1)} %param.11, bf16[256,64,128]{2,1,0:T(8,128)(2,1)} %gather_fusion, pred[256]{0:T(512)(128)(4,1)S(1)} %compare_and_fusion), kind=kOutput, calls=%fused_computation.2 | convolution fusion | flops 540803072 | bytes 13631744 | tf_op jit(solution)/shard_map/kcv,kvw->kcw/dot_general | solution.py:50
  323.3 1.4 fusion.7
  (10 shorter events, 0.3 us)
Async XLA Ops:
  7.2 219.6 %copy-start = (bf16[2,128,128]{2,1,0:T(8,128)(2,1)S(1)}, bf16[2,128,128]{2,1,0:T(8,128)(2,1)}, u32[]{:S(2)}) copy-start(bf16[2,128,128]{2,1,0:T(8,128)(2,1)} %param.10) | copy-start | bytes 196612
  7.2 22.3 %copy-start.2 = (bf16[8,128,128]{2,1,0:T(8,128)(2,1)S(1)}, bf16[8,128,128]{2,1,0:T(8,128)(2,1)}, u32[]{:S(2)}) copy-start(bf16[8,128,128]{2,1,0:T(8,128)(2,1)} %param.9) | copy-start | bytes 786436
  7.2 219.5 %reduce-scatter.2.cloned.1.call-start = ((), (), s32[]{:S(2)}) async-start(), calls=%async_computation.1 | async-start | bytes 4259840 | tf_op jit(solution)/shard_map/reduce_scatter | solution.py:34
  7.2 7.4 %collective-permute-start = (bf16[8,128,128]{2,1,0:T(8,128)(2,1)}, bf16[8,128,128]{2,1,0:T(8,128)(2,1)S(1)}, u32[]{:S(2)}, u32[]{:S(2)}) collective-permute-start(bf16[8,128,128]{2,1,0:T(8,128)(2,1)} %param.9), channel_id=1, source_target_pairs={{0,1},{1,2},{2,3},{3,0},{4,5},{5,6},{6,7},{7,4},{8,9},{9,10},{10,1... | collective-permute-start | bytes 786440 | tf_op jit(solution)/shard_map/ppermute | solution.py:12
  14.6 7.2 %collective-permute-start.1 = (bf16[8,128,128]{2,1,0:T(8,128)(2,1)S(1)}, bf16[8,128,128]{2,1,0:T(8,128)(2,1)S(1)}, u32[]{:S(2)}, u32[]{:S(2)}) collective-permute-start(bf16[8,128,128]{2,1,0:T(8,128)(2,1)S(1)} %collective-permute-done), channel_id=1, source_target_pairs={{0,1},{1,2},{2,3},{3,0},{4,5},{5,6},{6,7},{7,4},{8,9},{9,10},{10,1... | collective-permute-start | bytes 786440 | tf_op jit(solution)/shard_map/ppermute | solution.py:12
  21.8 6.4 %collective-permute-start.2 = (bf16[8,128,128]{2,1,0:T(8,128)(2,1)S(1)}, bf16[8,128,128]{2,1,0:T(8,128)(2,1)S(1)}, u32[]{:S(2)}, u32[]{:S(2)}) collective-permute-start(bf16[8,128,128]{2,1,0:T(8,128)(2,1)S(1)} %collective-permute-done.1), channel_id=1, source_target_pairs={{0,1},{1,2},{2,3},{3,0},{4,5},{5,6},{6,7},{7,4},{8,9},{9,10},{10,1... | collective-permute-start | bytes 786440 | tf_op jit(solution)/shard_map/ppermute | solution.py:12
  23.3 6.2 %copy-start.1 = (f32[32,64,128]{2,1,0:T(8,128)S(1)}, f32[32,64,128]{2,1,0:T(8,128)}, u32[]{:S(2)}) copy-start(f32[32,64,128]{2,1,0:T(8,128)} %param.7) | copy-start | bytes 3145732
  81.8 144.9 %copy-start.3 = (f32[2,64,128]{2,1,0:T(8,128)S(1)}, f32[2,64,128]{2,1,0:T(8,128)}, u32[]{:S(2)}) copy-start(f32[2,64,128]{2,1,0:T(8,128)} %param.8) | copy-start | bytes 196612
  81.8 229.7 %all-gather.2.cloned.1.call-start = ((), (), s32[]{:S(2)}) async-start(), calls=%async_computation.2 | async-start | bytes 2129920 | tf_op jit(solution)/shard_map/all_gather | solution.py:48
Sparse Core Ops, SparseCore 0:
  82.0 144.7 reduce-scatter.1
  230.5 81.0 all-gather.1
